TPU v7x, 128 devices: a whole 4x4x4 slice. The times are simulated.
128 devices in a mesh: gx: 16 (over y, x_hi, core), gy: 8 (over z, x_lo).
Axes of the slice: x: 4 (x_hi: 2, x_lo: 2; x = x_hi * 2 + x_lo), y: 4, z: 4, core: 2. Of those that a mesh axis runs over, the one named last changes fastest.
Arguments:
- obj: float32 [2, 4096, 8192], P(None, 'gy', 'gx'), may hold values from -6 to 6
- probe: float32 [2, 256, 256], replicated, may hold values from -6 to 6
- intensity: float32 [2048, 256, 256], P(('gx', 'gy')), may hold values from 0.1 to 4
- dest: int32 [2048, 1], P(('gx', 'gy')), may hold values from 0 to 15; in each aligned block of 16 rows (0 to 15, 16 to 31, ...) at most 2 rows name the same one
- offsets: int32 [2048, 2], P(('gx', 'gy')), may hold values from 0 to 511
Outputs:
- new_obj: float32 [2, 4096, 8192], P(None, 'gy', 'gx')
Inputs may be any that keep to these rules, and one draw needn't show every extreme that they name: `dest`: in each aligned block of 16 rows (the frames of one device) no tile column is named by more than 2 rows.
All inputs are finite; a program needn't handle non-finite values.
Results may differ from a plain program's by a relative error of at most 0.006.
Values may be sent and summed in bfloat16 or wider, within the bound.
No kernel may reach another device: no remote copies, remote signals or barrier semaphores. Data moves between devices by JAX's collectives and lax.ppermute only.
A program may use at most 192 MiB of HBM per device.

v0:
```python
import functools
import math

import jax
import jax.numpy as jnp
import numpy as np
from jax import lax
from jax.experimental import pallas as pl
from jax.experimental.pallas import tpu as pltpu
from jax.sharding import PartitionSpec as P

CAP = 2
FRAME = 256
HALF = 128
TILE = 512
EXTENT = TILE + 2 * HALF
PANELS = EXTENT // 128
NOTE_ROWS = 16
GROUP = 4
BF16 = jnp.bfloat16
F32 = jnp.float32


def table_blocks():
    index = np.arange(FRAME)[:, None] * np.arange(FRAME)[None, :] % FRAME
    angle = index.astype(np.float32) * np.float32(2.0 * math.pi / FRAME)
    scale = np.float32(1.0 / math.sqrt(FRAME))
    re = (np.cos(angle) * scale).astype(BF16)
    im = (-np.sin(angle) * scale).astype(BF16)
    blocks = []
    for parity in (0, 1):
        c = re[:HALF, parity::2]
        s = im[:HALF, parity::2]
        fwd_right = np.block([[c, s], [-s, c]])
        fwd_left = fwd_right.T
        inv_right = np.block([[c.T, -s.T], [s.T, c.T]])
        inv_left = inv_right.T
        blocks.append([fwd_right, fwd_left, inv_right, inv_left])
    return np.stack([blocks[p][i] for i in range(4) for p in (0, 1)]).astype(BF16)


def deinterleave():
    perm = np.zeros((FRAME, FRAME), np.float32)
    for j in range(HALF):
        perm[2 * j, j] = 1.0
        perm[2 * j + 1, HALF + j] = 1.0
    return perm.astype(BF16)


def dot(a, b):
    return jnp.dot(a, b, preferred_element_type=F32)


def prep_kernel(
    where_ref, inten_ref, perm_ref, first_ref, second_ref, stage, split, notes, ranks, sems
):
    step = pl.program_id(0)
    count = pl.num_programs(0)
    per = inten_ref.shape[0]
    groups = first_ref.shape[0]
    slot = step % 2

    def notes_copy():
        return pltpu.make_async_copy(
            notes, first_ref.at[:, pl.ds(2 * FRAME, NOTE_ROWS), :], sems.at[2 * per]
        )

    @pl.when(step == 0)
    def _():
        lane = lax.broadcasted_iota(jnp.int32, (groups, 128), 1)
        owner = lax.broadcasted_iota(jnp.int32, (groups, 128), 0)
        note = jnp.zeros((groups, 128), jnp.int32)
        for g in range(groups):
            ranks[per * count + g] = 0
        for f in range(per * count):
            mine = where_ref[f]
            rank = ranks[per * count + mine]
            ranks[f] = rank
            ranks[per * count + mine] = rank + 1
            row, col = where_ref[per * count + f], where_ref[2 * per * count + f]
            at = lane - 5 * rank
            value = jnp.where(at == 0, row // 16, jnp.where(at == 1, row % 16, 0))
            value += jnp.where(at == 2, col // 16, jnp.where(at == 3, col % 16, 0))
            value += jnp.where(at == 4, 1, 0)
            note = jnp.where(owner == mine, note + value, note)
        notes[...] = jnp.broadcast_to(note.astype(F32)[:, None, :], notes.shape).astype(BF16)
        notes_copy().start()

    for i in range(per):

        @pl.when(step >= 2)
        def _():
            pltpu.make_async_copy(
                stage.at[slot, i], second_ref.at[0], sems.at[slot * per + i]
            ).wait()

    for i in range(per):
        for h in range(2):
            split[i, h] = jnp.sqrt(inten_ref[i, :, 128 * h : 128 * h + 128])
        rows = [
            jnp.concatenate([split[i, h, pl.ds(p, HALF, 2), :] for h in range(2)], axis=1)
            for p in range(2)
        ]
        amp = jnp.concatenate(rows, axis=0).astype(BF16)
        cols = dot(amp, perm_ref[...]).astype(BF16)
        stage[slot, i, 0:FRAME, :] = cols[:, :128]
        stage[slot, i, FRAME : 2 * FRAME, :] = cols[:, 128:]
    for i in range(per):
        f = step * per + i
        mine = where_ref[f]
        rank = ranks[f]

        @pl.when(rank == 0)
        def _():
            pltpu.make_async_copy(
                stage.at[slot, i],
                first_ref.at[mine, pl.ds(0, 2 * FRAME), :],
                sems.at[slot * per + i],
            ).start()

        @pl.when(rank != 0)
        def _():
            pltpu.make_async_copy(
                stage.at[slot, i], second_ref.at[mine], sems.at[slot * per + i]
            ).start()

    @pl.when(step == count - 1)
    def _():
        notes_copy().wait()
        for s in range(2):
            for i in range(per):
                pltpu.make_async_copy(
                    stage.at[s, i], second_ref.at[0], sems.at[s * per + i]
                ).wait()


def prep(where, intensity, groups):
    frames = intensity.shape[0]
    per = 4
    return pl.pallas_call(
        prep_kernel,
        grid_spec=pltpu.PrefetchScalarGridSpec(
            num_scalar_prefetch=1,
            grid=(frames // per,),
            in_specs=[
                pl.BlockSpec((per, FRAME, FRAME), lambda s, w: (s, 0, 0)),
                pl.BlockSpec((FRAME, FRAME), lambda s, w: (0, 0)),
            ],
            out_specs=[pl.BlockSpec(memory_space=pl.ANY)] * 2,
            scratch_shapes=[
                pltpu.VMEM((2, per, 2 * FRAME, 128), BF16),
                pltpu.VMEM((per, 2, FRAME, 128), F32),
                pltpu.VMEM((groups, NOTE_ROWS, 128), BF16),
                pltpu.SMEM((frames + groups,), jnp.int32),
                pltpu.SemaphoreType.DMA((2 * per + 1,)),
            ],
        ),
        out_shape=[
            jax.ShapeDtypeStruct((groups, 2 * FRAME + NOTE_ROWS, 128), BF16),
            jax.ShapeDtypeStruct((groups, 2 * FRAME, 128), BF16),
        ],
        compiler_params=pltpu.CompilerParams(vmem_limit_bytes=56 << 20),
        cost_estimate=pl.CostEstimate(
            flops=frames * 2 * FRAME**3, bytes_accessed=frames * FRAME * FRAME * 6, transcendentals=0
        ),
        name="prep",
    )(where, intensity, jnp.asarray(deinterleave()))


def tile_copies(obj_hbm, ext_ref, sems):
    return [
        pltpu.make_async_copy(
            obj_hbm.at[part, :, pl.ds(128 * j, 128)],
            ext_ref.at[part, j + 1, pl.ds(HALF, TILE), :],
            sems.at[1 + part * (TILE // 128) + j],
        )
        for part in range(2)
        for j in range(TILE // 128)
    ]


def set_halo(north_ref, south_ref, west_ref, east_ref, ext_ref):
    for part in range(2):
        ext_ref[part, 0] = west_ref[part].astype(F32)
        ext_ref[part, PANELS - 1] = east_ref[part].astype(F32)
        for j in range(TILE // 128):
            lanes = slice(128 * j, 128 * j + 128)
            ext_ref[part, j + 1, 0:HALF, :] = north_ref[part, :, lanes].astype(F32)
            ext_ref[part, j + 1, HALF + TILE :, :] = south_ref[part, :, lanes].astype(F32)


def rows_of(m, p=0, height=FRAME):
    return slice(FRAME * m + HALF * p, FRAME * m + HALF * p + height)


def forward(places, probe_ref, table_ref, ext_ref, xs, gs, take):
    members = range(len(places))
    lane = lax.broadcasted_iota(jnp.int32, (FRAME, 128), 1)
    for m in members:
        row, col, live = places[m]
        panel = col // 128
        shift = col % 128
        back_shift = (128 - shift) % 128
        keep = lane < 128 - shift

        def cut(part):
            rolled = [
                pltpu.roll(ext_ref[part, panel + i, pl.ds(row, FRAME), :], back_shift, 1)
                for i in range(3)
            ]
            return [jnp.where(keep, rolled[i], rolled[i + 1]) for i in range(2)]

        patch_re = cut(0)
        patch_im = cut(1)
        ex_re, ex_im = [], []
        for h in range(2):
            lanes = slice(128 * h, 128 * h + 128)
            pr = probe_ref[0, :, lanes]
            pi = probe_ref[1, :, lanes]
            ex_re.append(pr * patch_re[h] - pi * patch_im[h])
            ex_im.append(pr * patch_im[h] + pi * patch_re[h])
        xs[0, rows_of(m), 0:128] = (ex_re[0] + ex_re[1]).astype(BF16)
        xs[0, rows_of(m), 128:256] = (ex_im[0] + ex_im[1]).astype(BF16)
        xs[1, rows_of(m), 0:128] = (ex_re[0] - ex_re[1]).astype(BF16)
        xs[1, rows_of(m), 128:256] = (ex_im[0] - ex_im[1]).astype(BF16)
    halves = [dot(xs[q], table_ref[q]) for q in range(2)]
    for m in members:
        for q in range(2):
            half = halves[q][rows_of(m)]
            top, bottom = half[:HALF], half[HALF:]
            lanes = slice(128 * q, 128 * q + 128)
            for p, fold in ((0, top + bottom), (1, top - bottom)):
                folded = fold.astype(BF16)
                gs[m, p, 0:HALF, lanes] = folded[:, :128]
                gs[m, p, HALF:, lanes] = folded[:, 128:]
    for m in members:
        for p in range(2):
            take(m, p, dot(table_ref[2 + p], gs[m, p]))


def update(m, p, far, amp_ref, ds):
    for q in range(2):
        lanes = slice(128 * q, 128 * q + 128)
        far_re, far_im = far[:HALF, lanes], far[HALF:, lanes]
        a = amp_ref[m, FRAME * q + HALF * p : FRAME * q + HALF * p + HALF, :].astype(F32)
        factor = a * lax.rsqrt(far_re * far_re + far_im * far_im + 1.0) - 1.0
        ds[q, rows_of(m, p, HALF), 0:128] = (far_re * factor).astype(BF16)
        ds[q, rows_of(m, p, HALF), 128:256] = (far_im * factor).astype(BF16)


def backward(places, probe_ref, table_ref, acc_ref, ds, ms):
    members = range(len(places))
    lane = lax.broadcasted_iota(jnp.int32, (HALF, 128), 1)
    evens = dot(ds[0], table_ref[4])
    odds = dot(ds[1], table_ref[5])
    for m in members:
        even, odd = evens[rows_of(m)], odds[rows_of(m)]
        for h, mid in ((0, (even + odd).astype(BF16)), (1, (even - odd).astype(BF16))):
            lanes = slice(128 * h, 128 * h + 128)
            for p in range(2):
                rows = slice(HALF * p, HALF * p + HALF)
                ms[m, p, 0:HALF, lanes] = mid[rows, :128]
                ms[m, p, HALF:, lanes] = mid[rows, 128:]
    for m in members:
        row, col, live = places[m]
        shift = col % 128
        panel = jnp.where(live > 0, col // 128, PANELS)
        even = dot(table_ref[6], ms[m, 0])
        odd = dot(table_ref[7], ms[m, 1])
        keep = lane < shift
        for v in range(2):
            back = even + odd if v == 0 else even - odd
            back_re, back_im = back[:HALF], back[HALF:]
            rows = slice(HALF * v, HALF * v + HALF)
            pr = probe_ref[0, rows]
            pi = probe_ref[1, rows]
            where = pl.ds(row + HALF * v, HALF)
            for part, term in ((0, pr * back_re + pi * back_im), (1, pr * back_im - pi * back_re)):
                left = pltpu.roll(term[:, :128], shift, 1)
                right = pltpu.roll(term[:, 128:], shift, 1)
                acc_ref[part, panel, where, :] += jnp.where(keep, 0.0, left)
                acc_ref[part, panel + 1, where, :] += jnp.where(keep, left, right)
                acc_ref[part, panel + 2, where, :] += jnp.where(keep, right, 0.0)


def places_of(meta_ref, rank, group):
    places = [[meta_ref[3 * rank + k, group * GROUP + m] for k in range(3)] for m in range(GROUP)]
    live = places[0][2]
    for place in places[1:]:
        live = live + place[2]
    return places, live > 0


def first_kernel(
    meta_ref, amp_ref, probe_ref, table_ref, north_ref, south_ref, west_ref, east_ref, obj_hbm,
    out_hbm, far_ref, ext_ref, acc_ref, sems, xs, gs, ds, ms,
):
    step = pl.program_id(0)
    groups = pl.num_programs(0) // 2

    def save():
        return pltpu.make_async_copy(acc_ref.at[:, pl.ds(0, PANELS)], out_hbm, sems.at[0])

    @pl.when(step == 0)
    def _():
        copies = tile_copies(obj_hbm, ext_ref, sems)
        for copy in copies:
            copy.start()
        acc_ref[:, 0:PANELS] = jnp.zeros_like(ext_ref)
        set_halo(north_ref, south_ref, west_ref, east_ref, ext_ref)
        for copy in copies:
            copy.wait()
        inner = slice(HALF, HALF + TILE)
        acc_ref[:, 1 : PANELS - 1, inner, :] = 2.0 * ext_ref[:, 1 : PANELS - 1, inner, :]

    places, live = places_of(meta_ref, 0, jnp.minimum(step, groups - 1))

    @pl.when(live & (step < groups))
    def _():
        def take(m, p, far):
            update(m, p, far, amp_ref, ds)

        forward(places, probe_ref, table_ref, ext_ref, xs, gs, take)
        backward(places, probe_ref, table_ref, acc_ref, ds, ms)

    @pl.when(step == groups - 1)
    def _():
        save().start()

    later, live = places_of(meta_ref, 1, jnp.maximum(step - groups, 0))

    @pl.when(live & (step >= groups))
    def _():
        def take(m, p, far):
            far_ref[m, p] = far.astype(BF16)

        forward(later, probe_ref, table_ref, ext_ref, xs, gs, take)

    @pl.when(step == pl.num_programs(0) - 1)
    def _():
        save().wait()


def last_kernel(
    meta_ref, amp_ref, far_ref, probe_ref, table_ref, start_hbm,
    west_ref, east_ref, top_ref, bottom_ref, inner_ref, acc_ref, start_ref, sems, ds, ms,
):
    step = pl.program_id(0)

    def load():
        return pltpu.make_async_copy(start_hbm, start_ref, sems.at[0])

    @pl.when(step == 0)
    def _():
        load().start()
        acc_ref[:, 0:PANELS] = jnp.zeros_like(start_ref)

    places, live = places_of(meta_ref, 1, step)

    @pl.when(live)
    def _():
        for m in range(GROUP):
            for p in range(2):
                update(m, p, far_ref[m, p].astype(F32), amp_ref, ds)
        backward(places, probe_ref, table_ref, acc_ref, ds, ms)

    @pl.when(step == pl.num_programs(0) - 1)
    def _():
        load().wait()

        def half_sum(part, panel, rows):
            return 0.5 * (acc_ref[part, panel, rows, :] + start_ref[part, panel, rows, :])

        for part in range(2):
            west_ref[part] = half_sum(part, 0, slice(0, EXTENT)).astype(BF16)
            east_ref[part] = half_sum(part, PANELS - 1, slice(0, EXTENT)).astype(BF16)
            for j in range(TILE // 128):
                lanes = slice(128 * j, 128 * j + 128)
                top_ref[part, :, lanes] = half_sum(part, j + 1, slice(0, HALF))
                inner_ref[part, :, lanes] = half_sum(part, j + 1, slice(HALF, HALF + TILE))
                bottom_ref[part, :, lanes] = half_sum(part, j + 1, slice(HALF + TILE, EXTENT))


def whole(shape):
    return pl.BlockSpec(shape, lambda s, m: (0,) * len(shape))


WIDE = (2, PANELS, EXTENT, 128)
SUMS = (2, PANELS + 3, EXTENT, 128)
FLAT = (2, GROUP * FRAME, FRAME)
DEEP = (GROUP, 2, FRAME, FRAME)


def run_first(meta, amps, probe, tabs, obj, north, south, west, east):
    groups = amps.shape[0] // GROUP
    return pl.pallas_call(
        first_kernel,
        grid_spec=pltpu.PrefetchScalarGridSpec(
            num_scalar_prefetch=1,
            grid=(2 * groups,),
            in_specs=[
                pl.BlockSpec(
                    (GROUP,) + amps.shape[1:], lambda s, m: (jnp.minimum(s, groups - 1), 0, 0)
                ),
                whole((2, FRAME, FRAME)),
                whole((8, FRAME, FRAME)),
                whole(north.shape),
                whole(south.shape),
                whole(west.shape),
                whole(east.shape),
                pl.BlockSpec(memory_space=pl.ANY),
            ],
            out_specs=[
                pl.BlockSpec(memory_space=pl.ANY),
                pl.BlockSpec(DEEP, lambda s, m: (jnp.maximum(s - groups, 0), 0, 0, 0)),
            ],
            scratch_shapes=[
                pltpu.VMEM(WIDE, F32),
                pltpu.VMEM(SUMS, F32),
                pltpu.SemaphoreType.DMA((1 + 2 * TILE // 128,)),
            ]
            + [pltpu.VMEM(shape, BF16) for shape in (FLAT, DEEP, FLAT, DEEP)],
        ),
        out_shape=[
            jax.ShapeDtypeStruct(WIDE, F32),
            jax.ShapeDtypeStruct((amps.shape[0], 2, FRAME, FRAME), BF16),
        ],
        compiler_params=pltpu.CompilerParams(vmem_limit_bytes=56 << 20),
        cost_estimate=pl.CostEstimate(
            flops=2 * amps.shape[0] * 16 * FRAME**3, bytes_accessed=24 << 20, transcendentals=0
        ),
        name="first",
    )(meta, amps, probe, tabs, north, south, west, east, obj)


def run_last(meta, amps, far, probe, tabs, start):
    groups = amps.shape[0] // GROUP

    def used(s, m):
        live = m[5, s * GROUP]
        for k in range(1, GROUP):
            live = live + m[5, s * GROUP + k]
        return jnp.where(live > 0, s, 0)

    shapes = [(2, EXTENT, 128)] * 2 + [(2, HALF, TILE)] * 2 + [(2, TILE, TILE)]
    return pl.pallas_call(
        last_kernel,
        grid_spec=pltpu.PrefetchScalarGridSpec(
            num_scalar_prefetch=1,
            grid=(groups,),
            in_specs=[
                pl.BlockSpec((GROUP,) + amps.shape[1:], lambda s, m: (used(s, m), 0, 0)),
                pl.BlockSpec(DEEP, lambda s, m: (used(s, m), 0, 0, 0)),
                whole((2, FRAME, FRAME)),
                whole((8, FRAME, FRAME)),
                pl.BlockSpec(memory_space=pl.ANY),
            ],
            out_specs=[whole(shape) for shape in shapes],
            scratch_shapes=[
                pltpu.VMEM(SUMS, F32),
                pltpu.VMEM(WIDE, F32),
                pltpu.SemaphoreType.DMA((1,)),
                pltpu.VMEM(FLAT, BF16),
                pltpu.VMEM(DEEP, BF16),
            ],
        ),
        out_shape=[jax.ShapeDtypeStruct(s, d) for s, d in zip(shapes, (BF16, BF16, F32, F32, F32))],
        compiler_params=pltpu.CompilerParams(vmem_limit_bytes=56 << 20),
        cost_estimate=pl.CostEstimate(
            flops=amps.shape[0] * 8 * FRAME**3, bytes_accessed=20 << 20, transcendentals=0
        ),
        name="last",
    )(meta, amps, far, probe, tabs, start)


def across_kernel(top_ref, bottom_ref, west_n, west_s, east_n, east_s, north_ref, south_ref):
    for base, west, east, out in (
        (top_ref, west_n, east_n, north_ref), (bottom_ref, west_s, east_s, south_ref)
    ):
        out[:, :, 0:HALF] = (base[:, :, 0:HALF] + west[...].astype(F32)).astype(BF16)
        out[:, :, HALF : TILE - HALF] = base[:, :, HALF : TILE - HALF].astype(BF16)
        out[:, :, TILE - HALF :] = (base[:, :, TILE - HALF :] + east[...].astype(F32)).astype(BF16)


def across(top, bottom, from_west, from_east):
    end = EXTENT // HALF - 1
    full = pl.BlockSpec((2, HALF, TILE), lambda i: (0, 0, 0))
    first = pl.BlockSpec((2, HALF, 128), lambda i: (0, 0, 0))
    last = pl.BlockSpec((2, HALF, 128), lambda i: (0, end, 0))
    return pl.pallas_call(
        across_kernel,
        grid=(1,),
        in_specs=[full, full, first, last, first, last],
        out_specs=[full, full],
        out_shape=[jax.ShapeDtypeStruct((2, HALF, TILE), BF16)] * 2,
        compiler_params=pltpu.CompilerParams(vmem_limit_bytes=10 << 20),
        name="across",
    )(top, bottom, from_west, from_west, from_east, from_east)


def sides_kernel(base_ref, west_ref, east_ref, out_ref):
    inner = slice(HALF, HALF + TILE)

    @pl.when(pl.program_id(0) == 0)
    def _():
        out_ref[...] = base_ref[...] + west_ref[:, inner, :].astype(F32)

    @pl.when(pl.program_id(0) == 1)
    def _():
        out_ref[...] = base_ref[...] + east_ref[:, inner, :].astype(F32)


def ends_kernel(base_ref, north_ref, south_ref, out_ref):
    @pl.when(pl.program_id(0) == 0)
    def _():
        out_ref[...] = base_ref[...] + north_ref[...].astype(F32)

    @pl.when(pl.program_id(0) == 1)
    def _():
        out_ref[...] = base_ref[...] + south_ref[...].astype(F32)


def add_pair(kernel, base, block, place, low, high):
    strip = pl.BlockSpec(low.shape, lambda i: (0, 0, 0))
    return pl.pallas_call(
        kernel,
        grid=(2,),
        in_specs=[pl.BlockSpec(block, place), strip, strip],
        out_specs=pl.BlockSpec(block, place),
        out_shape=jax.ShapeDtypeStruct(base.shape, F32),
        input_output_aliases={0: 0},
        compiler_params=pltpu.CompilerParams(vmem_limit_bytes=10 << 20),
        name="ends",
    )(base, low, high)


def shifted(value, axis, by):
    size = lax.axis_size(axis)
    pairs = [(i, i + by) for i in range(size) if 0 <= i + by < size]
    return lax.ppermute(value, axis, pairs)


def body(obj, probe, intensity, dest, offsets):
    groups = lax.axis_size("gx")
    sends = prep(jnp.concatenate([dest.T, offsets.T]).reshape(-1), intensity, groups)
    north = shifted(obj[:, TILE - HALF :, :].astype(BF16), "gy", 1)
    south = shifted(obj[:, :HALF, :].astype(BF16), "gy", -1)
    routed = functools.partial(
        lax.all_to_all, axis_name="gx", split_axis=0, concat_axis=0, tiled=True
    )
    first, north, south = lax.optimization_barrier((sends[0], north, south))
    amps = routed(first)

    def column(lo, hi):
        own = obj[:, :, lo:hi].astype(BF16)
        return jnp.concatenate([north[:, :, lo:hi], own, south[:, :, lo:hi]], axis=1)

    west = shifted(column(TILE - HALF, TILE), "gx", 1)
    east = shifted(column(0, HALF), "gx", -1)
    west, east, rest = lax.optimization_barrier((west, east, sends[1]))
    more = routed(rest)
    tabs = jnp.asarray(table_blocks())
    notes = amps[:, 2 * FRAME, :10].astype(jnp.int32).T
    meta = jnp.stack(
        [
            notes[5 * r] * 16 + notes[5 * r + 1] if k == 0 else
            notes[5 * r + 2] * 16 + notes[5 * r + 3] if k == 1 else notes[5 * r + 4]
            for r in range(CAP) for k in range(3)
        ]
    )
    acc, far = run_first(meta, amps, probe, tabs, obj, north, south, west, east)
    west, east, top, bottom, inner = run_last(meta, more, far, probe, tabs, acc)
    from_west = shifted(east, "gx", 1)
    from_east = shifted(west, "gx", -1)
    to_north, to_south = across(top, bottom, from_west, from_east)
    from_north = shifted(to_south, "gy", 1)
    from_south = shifted(to_north, "gy", -1)
    steps = TILE // HALF - 1
    inner = add_pair(
        sides_kernel, inner, (2, TILE, HALF), lambda i: (0, 0, steps * i), from_west, from_east
    )
    return add_pair(
        ends_kernel, inner, (2, HALF, TILE), lambda i: (0, steps * i, 0), from_north, from_south
    )


def solution(mesh):
    placed = (
        P(None, "gy", "gx"),
        P(),
        P(("gx", "gy"), None, None),
        P(("gx", "gy"), None),
        P(("gx", "gy"), None),
    )
    return jax.shard_map(
        body, mesh=mesh, in_specs=placed, out_specs=P(None, "gy", "gx"), check_vma=False
    )
```

profile of v0, /device:TPU:71, one launch (start us, length us, event | category | flops | bytes accessed | tf_op | source)
XLA Modules:
  0.0 142.7 jit_solution(2456407677126536521)
XLA Ops:
  0.0 0.0 copy-start.6
  0.0 0.0 copy-start.7
  0.0 1.8 %convert.8 = bf16[2,512,512]{2,1,0:T(8,128)(2,1)S(1)} convert(f32[2,512,512]{2,1,0:T(8,128)} %obj_hbm.1) | non-fusion elementwise | flops 524288 | bytes 3145728 | tf_op jit(solution)/shard_map/convert.5
  1.8 2.5 %collective-permute-start.1 = (bf16[2,128,512]{2,1,0:T(8,128)(2,1)S(1)}, bf16[2,128,512]{2,1,0:T(8,128)(2,1)S(1)}, u32[]{:S(2)}, u32[]{:S(2)}) collective-permute-start(bf16[2,128,512]{2,1,0:T(8,128)(2,1)S(1)} %get-tuple-element.41), channel_id=1, source_target_pairs={{1,0},{2,1},{3,2},{4,3},{5,4},{6,5},{7,6},{9,8},{10,9},{11,10},{12... | collective-permute-start | bytes 786440 | tf_op jit(solution)/shard_map/ppermute | solution.py:540
  4.3 3.7 %collective-permute-start = (bf16[2,128,512]{2,1,0:T(8,128)(2,1)S(1)}, bf16[2,128,512]{2,1,0:T(8,128)(2,1)S(1)}, u32[]{:S(2)}, u32[]{:S(2)}) collective-permute-start(bf16[2,128,512]{2,1,0:T(8,128)(2,1)S(1)} %get-tuple-element.42), channel_id=1, source_target_pairs={{0,1},{1,2},{2,3},{3,4},{4,5},{5,6},{6,7},{8,9},{9,10},{10,11},{11... | collective-permute-start | bytes 786440 | tf_op jit(solution)/shard_map/ppermute | solution.py:540
  8.0 0.0 copy-done.6
  8.0 0.0 copy-done.7
  8.0 0.6 reshape.5.where_ref
  8.6 6.1 %prep.1 = (bf16[16,528,128]{2,1,0:T(8,128)(2,1)}, bf16[16,512,128]{2,1,0:T(8,128)(2,1)}) custom-call(s32[48]{0:T(128)} %reshape.5.where_ref, f32[16,256,256]{2,1,0:T(8,128)} %inten_ref.1, bf16[256,256]{1,0:T(8,128)(2,1)} %constant.6.clone.perm_ref), custom_call_target="tpu_custom_call" | custom-call | flops 536870912 | bytes 6291456 | tf_op jit(solution)/shard_map/prep/pallas_call | solution.py:140
  14.8 0.0 collective-permute-done.1.south_ref
  14.8 0.0 copy-start.4
  14.8 1.2 collective-permute-done.north_ref
  16.0 0.0 copy-start.5
  16.0 0.7 copy-done.5
  16.7 8.6 %all-to-all-start = ((bf16[16,528,128]{2,1,0:T(8,128)(2,1)}), bf16[16,528,128]{2,1,0:T(8,128)(2,1)S(1)}, u32[]{:S(2)}, u32[]{:S(2)}) async-start(bf16[16,528,128]{2,1,0:T(8,128)(2,1)} %get-tuple-element.23), calls=%async_computation | async-start | bytes 4325376 | tf_op jit(solution)/shard_map/all_to_all | solution.py:552
  25.4 0.1 fusion
  25.5 0.0 copy-done.4
  25.5 0.9 fusion.2
  26.4 3.3 %collective-permute-start.2 = (bf16[2,768,128]{2,1,0:T(8,128)(2,1)S(1)}, bf16[2,768,128]{2,1,0:T(8,128)(2,1)S(1)}, u32[]{:S(2)}, u32[]{:S(2)}) collective-permute-start(bf16[2,768,128]{2,1,0:T(8,128)(2,1)S(1)} %pad_maximum_fusion), channel_id=1, source_target_pairs={{0,8},{8,16},{16,24},{24,32},{32,40},{40,48},{48,56},{56,64},{64,7... | collective-permute-start | bytes 1179656 | tf_op jit(solution)/shard_map/ppermute | solution.py:540
  29.8 1.9 %collective-permute-start.3 = (bf16[2,768,128]{2,1,0:T(8,128)(2,1)S(1)}, bf16[2,768,128]{2,1,0:T(8,128)(2,1)S(1)}, u32[]{:S(2)}, u32[]{:S(2)}) collective-permute-start(bf16[2,768,128]{2,1,0:T(8,128)(2,1)S(1)} %pad_maximum_fusion.1), channel_id=1, source_target_pairs={{8,0},{16,8},{24,16},{32,24},{40,32},{48,40},{56,48},{64,56},{72,6... | collective-permute-start | bytes 1179656 | tf_op jit(solution)/shard_map/ppermute | solution.py:540
  31.7 27.1 %collective-permute-done.2.west_ref = bf16[2,768,128]{2,1,0:T(8,128)(2,1)S(1)} collective-permute-done((bf16[2,768,128]{2,1,0:T(8,128)(2,1)S(1)}, bf16[2,768,128]{2,1,0:T(8,128)(2,1)S(1)}, u32[]{:S(2)}, u32[]{:S(2)}) %collective-permute-start.2) | collective-permute-done | bytes 393248 | tf_op jit(solution)/shard_map/ppermute | solution.py:540
  58.8 0.0 copy-start.8
  58.8 0.6 collective-permute-done.3.east_ref
  59.4 0.0 all-to-all-done.amp_ref
  59.4 1.4 copy-done.3
  60.8 7.2 %all-to-all-start.1 = ((bf16[16,512,128]{2,1,0:T(8,128)(2,1)}), bf16[16,512,128]{2,1,0:T(8,128)(2,1)S(1)}, u32[]{:S(2)}, u32[]{:S(2)}) async-start(bf16[16,512,128]{2,1,0:T(8,128)(2,1)} %get-tuple-element.27), calls=%async_computation.1 | async-start | bytes 4194304 | tf_op jit(solution)/shard_map/all_to_all | solution.py:561
  67.9 0.8 slice.82
  68.7 0.1 copy.13
  68.8 0.6 stack.2.meta_ref
  69.4 0.0 copy-done.8
  69.4 0.0 copy-done.9
  69.4 24.1 %first.1 = (f32[2,6,768,128]{3,2,1,0:T(8,128)}, bf16[16,2,256,256]{3,2,1,0:T(8,128)(2,1)}) custom-call(s32[6,16]{1,0:T(8,128)} %stack.2.meta_ref, bf16[16,528,128]{2,1,0:T(8,128)(2,1)} %copy-done.3, f32[2,256,256]{2,1,0:T(8,128)} %probe_ref.3, bf16[8,256,256]{2,1,0:T(8,128)(2,1)} %constant.7.clone.table_ref, bf16[2,128,512]{2,1,0:T(8,128)(2,1)} %copy-done.5, ...), custom_call_target="tpu_custom_call" | custom-call | flops 8589934592 | bytes 25165824 | tf_op jit(solution)/shard_map/first/pallas_call | solution.py:396
  93.6 1.0 all-to-all-done.1.amp_ref
  94.5 1.3 copy-done.2
  95.8 13.2 %last.1 = (bf16[2,768,128]{2,1,0:T(8,128)(2,1)}, bf16[2,768,128]{2,1,0:T(8,128)(2,1)}, f32[2,128,512]{2,1,0:T(8,128)}, f32[2,128,512]{2,1,0:T(8,128)}, f32[2,512,512]{2,1,0:T(8,128)}) custom-call(s32[6,16]{1,0:T(8,128)} %stack.2.meta_ref, bf16[16,512,128]{2,1,0:T(8,128)(2,1)} %copy-done.2, bf16[16,2,256,256]{3,2,1,0:T(8,128)(2,1)} %get-tuple-element.30.far_ref, ...), custom_call_target="tpu_custom_call" | custom-call | flops 2147483648 | bytes 20971520 | tf_op jit(solution)/shard_map/last/pallas_call | solution.py:446
  109.1 1.9 %collective-permute-start.4 = (bf16[2,768,128]{2,1,0:T(8,128)(2,1)}, bf16[2,768,128]{2,1,0:T(8,128)(2,1)S(1)}, u32[]{:S(2)}, u32[]{:S(2)}) collective-permute-start(bf16[2,768,128]{2,1,0:T(8,128)(2,1)} %get-tuple-element.33), channel_id=1, source_target_pairs={{0,8},{8,16},{16,24},{24,32},{32,40},{40,48},{48,56},{56,64},{64,7... | collective-permute-start | bytes 1179656 | tf_op jit(solution)/shard_map/ppermute | solution.py:540
  111.0 2.4 %collective-permute-start.5 = (bf16[2,768,128]{2,1,0:T(8,128)(2,1)}, bf16[2,768,128]{2,1,0:T(8,128)(2,1)S(1)}, u32[]{:S(2)}, u32[]{:S(2)}) collective-permute-start(bf16[2,768,128]{2,1,0:T(8,128)(2,1)} %get-tuple-element.34), channel_id=1, source_target_pairs={{8,0},{16,8},{24,16},{32,24},{40,32},{48,40},{56,48},{64,56},{72,6... | collective-permute-start | bytes 1179656 | tf_op jit(solution)/shard_map/ppermute | solution.py:540
  113.4 2.6 %collective-permute-done.4.west_ref.west_n.west_s = bf16[2,768,128]{2,1,0:T(8,128)(2,1)S(1)} collective-permute-done((bf16[2,768,128]{2,1,0:T(8,128)(2,1)}, bf16[2,768,128]{2,1,0:T(8,128)(2,1)S(1)}, u32[]{:S(2)}, u32[]{:S(2)}) %collective-permute-start.4) | collective-permute-done | bytes 393248 | tf_op jit(solution)/shard_map/ppermute | solution.py:540
  116.0 6.7 %collective-permute-done.5.east_ref.east_n.east_s = bf16[2,768,128]{2,1,0:T(8,128)(2,1)S(1)} collective-permute-done((bf16[2,768,128]{2,1,0:T(8,128)(2,1)}, bf16[2,768,128]{2,1,0:T(8,128)(2,1)S(1)}, u32[]{:S(2)}, u32[]{:S(2)}) %collective-permute-start.5) | collective-permute-done | bytes 393248 | tf_op jit(solution)/shard_map/ppermute | solution.py:540
  122.7 1.0 copy-done
  123.8 1.0 copy-done.1
  124.8 0.1 across.1
  124.9 3.7 %collective-permute-start.6 = (bf16[2,128,512]{2,1,0:T(8,128)(2,1)S(1)}, bf16[2,128,512]{2,1,0:T(8,128)(2,1)S(1)}, u32[]{:S(2)}, u32[]{:S(2)}) collective-permute-start(bf16[2,128,512]{2,1,0:T(8,128)(2,1)S(1)} %get-tuple-element.37), channel_id=1, source_target_pairs={{0,1},{1,2},{2,3},{3,4},{4,5},{5,6},{6,7},{8,9},{9,10},{10,11},{11... | collective-permute-start | bytes 786440 | tf_op jit(solution)/shard_map/ppermute | solution.py:540
  128.6 1.9 %collective-permute-start.7 = (bf16[2,128,512]{2,1,0:T(8,128)(2,1)S(1)}, bf16[2,128,512]{2,1,0:T(8,128)(2,1)S(1)}, u32[]{:S(2)}, u32[]{:S(2)}) collective-permute-start(bf16[2,128,512]{2,1,0:T(8,128)(2,1)S(1)} %get-tuple-element.38), channel_id=1, source_target_pairs={{1,0},{2,1},{3,2},{4,3},{5,4},{6,5},{7,6},{9,8},{10,9},{11,10},{12... | collective-permute-start | bytes 786440 | tf_op jit(solution)/shard_map/ppermute | solution.py:540
  130.6 2.1 %ends.2.base_ref = f32[2,512,512]{2,1,0:T(8,128)} custom-call(f32[2,512,512]{2,1,0:T(8,128)} %get-tuple-element.32.base_ref, bf16[2,768,128]{2,1,0:T(8,128)(2,1)S(1)} %collective-permute-done.4.west_ref.west_n.west_s, bf16[2,768,128]{2,1,0:T(8,128)(2,1)S(1)} %collective-permute-done.5.east_ref.east_n.east_s), custom_call_target="tpu_custom_call", output_to_operand_aliasing={{}: (0, {})} | custom-call | tf_op jit(solution)/shard_map/ends/pallas_call | solution.py:525
  132.6 2.5 %collective-permute-done.6.north_ref = bf16[2,128,512]{2,1,0:T(8,128)(2,1)S(1)} collective-permute-done((bf16[2,128,512]{2,1,0:T(8,128)(2,1)S(1)}, bf16[2,128,512]{2,1,0:T(8,128)(2,1)S(1)}, u32[]{:S(2)}, u32[]{:S(2)}) %collective-permute-start.6) | collective-permute-done | bytes 262176 | tf_op jit(solution)/shard_map/ppermute | solution.py:540
  135.2 5.5 %collective-permute-done.7.south_ref = bf16[2,128,512]{2,1,0:T(8,128)(2,1)S(1)} collective-permute-done((bf16[2,128,512]{2,1,0:T(8,128)(2,1)S(1)}, bf16[2,128,512]{2,1,0:T(8,128)(2,1)S(1)}, u32[]{:S(2)}, u32[]{:S(2)}) %collective-permute-start.7) | collective-permute-done | bytes 262176 | tf_op jit(solution)/shard_map/ppermute | solution.py:540
  140.7 2.1 %ends.3 = f32[2,512,512]{2,1,0:T(8,128)} custom-call(f32[2,512,512]{2,1,0:T(8,128)} %ends.2.base_ref, bf16[2,128,512]{2,1,0:T(8,128)(2,1)S(1)} %collective-permute-done.6.north_ref, bf16[2,128,512]{2,1,0:T(8,128)(2,1)S(1)} %collective-permute-done.7.south_ref), custom_call_target="tpu_custom_call", output_to_operand_aliasing={{}: (0, {})} | custom-call | tf_op jit(solution)/shard_map/ends/pallas_call | solution.py:525
  (11 shorter events, 0.1 us)
Async XLA Ops:
  0.0 8.0 %copy-start.6 = (s32[16,2]{0,1:T(2,128)S(1)}, s32[16,2]{0,1:T(2,128)}, u32[]{:S(2)}) copy-start(s32[16,2]{0,1:T(2,128)} %param.11) | copy-start | bytes 388
  0.0 8.0 %copy-start.7 = (s32[16,1]{0,1:T(1,128)S(1)}, s32[16,1]{0,1:T(1,128)}, u32[]{:S(2)}) copy-start(s32[16,1]{0,1:T(1,128)} %param.10) | copy-start | bytes 196
  1.8 13.0 %collective-permute-start.1 = (bf16[2,128,512]{2,1,0:T(8,128)(2,1)S(1)}, bf16[2,128,512]{2,1,0:T(8,128)(2,1)S(1)}, u32[]{:S(2)}, u32[]{:S(2)}) collective-permute-start(bf16[2,128,512]{2,1,0:T(8,128)(2,1)S(1)} %get-tuple-element.41), channel_id=1, source_target_pairs={{1,0},{2,1},{3,2},{4,3},{5,4},{6,5},{7,6},{9,8},{10,9},{11,10},{12... | collective-permute-start | bytes 786440 | tf_op jit(solution)/shard_map/ppermute | solution.py:540
  4.3 11.8 %collective-permute-start = (bf16[2,128,512]{2,1,0:T(8,128)(2,1)S(1)}, bf16[2,128,512]{2,1,0:T(8,128)(2,1)S(1)}, u32[]{:S(2)}, u32[]{:S(2)}) collective-permute-start(bf16[2,128,512]{2,1,0:T(8,128)(2,1)S(1)} %get-tuple-element.42), channel_id=1, source_target_pairs={{0,1},{1,2},{2,3},{3,4},{4,5},{5,6},{6,7},{8,9},{9,10},{10,11},{11... | collective-permute-start | bytes 786440 | tf_op jit(solution)/shard_map/ppermute | solution.py:540
  14.8 10.7 %copy-start.4 = (bf16[2,128,512]{2,1,0:T(8,128)(2,1)}, bf16[2,128,512]{2,1,0:T(8,128)(2,1)S(1)}, u32[]{:S(2)}) copy-start(bf16[2,128,512]{2,1,0:T(8,128)(2,1)S(1)} %collective-permute-done.1.south_ref) | copy-start | bytes 786436
  16.0 0.7 copy-start.5
  16.7 42.7 %all-to-all-start = ((bf16[16,528,128]{2,1,0:T(8,128)(2,1)}), bf16[16,528,128]{2,1,0:T(8,128)(2,1)S(1)}, u32[]{:S(2)}, u32[]{:S(2)}) async-start(bf16[16,528,128]{2,1,0:T(8,128)(2,1)} %get-tuple-element.23), calls=%async_computation | async-start | bytes 4325376 | tf_op jit(solution)/shard_map/all_to_all | solution.py:552
  26.4 32.4 %collective-permute-start.2 = (bf16[2,768,128]{2,1,0:T(8,128)(2,1)S(1)}, bf16[2,768,128]{2,1,0:T(8,128)(2,1)S(1)}, u32[]{:S(2)}, u32[]{:S(2)}) collective-permute-start(bf16[2,768,128]{2,1,0:T(8,128)(2,1)S(1)} %pad_maximum_fusion), channel_id=1, source_target_pairs={{0,8},{8,16},{16,24},{24,32},{32,40},{40,48},{48,56},{56,64},{64,7... | collective-permute-start | bytes 1179656 | tf_op jit(solution)/shard_map/ppermute | solution.py:540
  29.8 29.6 %collective-permute-start.3 = (bf16[2,768,128]{2,1,0:T(8,128)(2,1)S(1)}, bf16[2,768,128]{2,1,0:T(8,128)(2,1)S(1)}, u32[]{:S(2)}, u32[]{:S(2)}) collective-permute-start(bf16[2,768,128]{2,1,0:T(8,128)(2,1)S(1)} %pad_maximum_fusion.1), channel_id=1, source_target_pairs={{8,0},{16,8},{24,16},{32,24},{40,32},{48,40},{56,48},{64,56},{72,6... | collective-permute-start | bytes 1179656 | tf_op jit(solution)/shard_map/ppermute | solution.py:540
  58.8 10.6 %copy-start.8 = (bf16[2,768,128]{2,1,0:T(8,128)(2,1)}, bf16[2,768,128]{2,1,0:T(8,128)(2,1)S(1)}, u32[]{:S(2)}) copy-start(bf16[2,768,128]{2,1,0:T(8,128)(2,1)S(1)} %collective-permute-done.2.west_ref) | copy-start | bytes 1179652
  59.4 10.0 %copy-start.9 = (bf16[2,768,128]{2,1,0:T(8,128)(2,1)}, bf16[2,768,128]{2,1,0:T(8,128)(2,1)S(1)}, u32[]{:S(2)}) copy-start(bf16[2,768,128]{2,1,0:T(8,128)(2,1)S(1)} %collective-permute-done.3.east_ref) | copy-start | bytes 1179652
  59.4 1.4 copy-start.3
  60.8 33.8 %all-to-all-start.1 = ((bf16[16,512,128]{2,1,0:T(8,128)(2,1)}), bf16[16,512,128]{2,1,0:T(8,128)(2,1)S(1)}, u32[]{:S(2)}, u32[]{:S(2)}) async-start(bf16[16,512,128]{2,1,0:T(8,128)(2,1)} %get-tuple-element.27), calls=%async_computation.1 | async-start | bytes 4194304 | tf_op jit(solution)/shard_map/all_to_all | solution.py:561
  94.5 1.3 copy-start.2
  109.1 6.9 %collective-permute-start.4 = (bf16[2,768,128]{2,1,0:T(8,128)(2,1)}, bf16[2,768,128]{2,1,0:T(8,128)(2,1)S(1)}, u32[]{:S(2)}, u32[]{:S(2)}) collective-permute-start(bf16[2,768,128]{2,1,0:T(8,128)(2,1)} %get-tuple-element.33), channel_id=1, source_target_pairs={{0,8},{8,16},{16,24},{24,32},{32,40},{40,48},{48,56},{56,64},{64,7... | collective-permute-start | bytes 1179656 | tf_op jit(solution)/shard_map/ppermute | solution.py:540
  111.0 11.7 %collective-permute-start.5 = (bf16[2,768,128]{2,1,0:T(8,128)(2,1)}, bf16[2,768,128]{2,1,0:T(8,128)(2,1)S(1)}, u32[]{:S(2)}, u32[]{:S(2)}) collective-permute-start(bf16[2,768,128]{2,1,0:T(8,128)(2,1)} %get-tuple-element.34), channel_id=1, source_target_pairs={{8,0},{16,8},{24,16},{32,24},{40,32},{48,40},{56,48},{64,56},{72,6... | collective-permute-start | bytes 1179656 | tf_op jit(solution)/shard_map/ppermute | solution.py:540
  122.7 1.0 copy-start
  123.8 1.0 copy-start.1
  124.9 10.2 %collective-permute-start.6 = (bf16[2,128,512]{2,1,0:T(8,128)(2,1)S(1)}, bf16[2,128,512]{2,1,0:T(8,128)(2,1)S(1)}, u32[]{:S(2)}, u32[]{:S(2)}) collective-permute-start(bf16[2,128,512]{2,1,0:T(8,128)(2,1)S(1)} %get-tuple-element.37), channel_id=1, source_target_pairs={{0,1},{1,2},{2,3},{3,4},{4,5},{5,6},{6,7},{8,9},{9,10},{10,11},{11... | collective-permute-start | bytes 786440 | tf_op jit(solution)/shard_map/ppermute | solution.py:540
  128.6 12.0 %collective-permute-start.7 = (bf16[2,128,512]{2,1,0:T(8,128)(2,1)S(1)}, bf16[2,128,512]{2,1,0:T(8,128)(2,1)S(1)}, u32[]{:S(2)}, u32[]{:S(2)}) collective-permute-start(bf16[2,128,512]{2,1,0:T(8,128)(2,1)S(1)} %get-tuple-element.38), channel_id=1, source_target_pairs={{1,0},{2,1},{3,2},{4,3},{5,4},{6,5},{7,6},{9,8},{10,9},{11,10},{12... | collective-permute-start | bytes 786440 | tf_op jit(solution)/shard_map/ppermute | solution.py:540
where the time goes:
time: 143 us
  Pallas kernels  47.8 us (33%)
  waiting for transfers between devices  47.2 us (33%)
  starting transfers between devices  37.2 us (26%)
  local copies, waits for them, and re-layouts  8.56 us (6%)
  other arithmetic  1.84 us (1%)
    ppermute x8, waiting for transfers between devices, shifted(): return lax.ppermute(value, axis, pairs)  46.2 us
    pallas_call x1, Pallas kernels, run_first(): pl.pallas_call(first_kernel, grid_spec=pltpu.PrefetchScalarGridSpec(num_s...  24.1 us
    ppermute x8, starting transfers between devices, shifted(): return lax.ppermute(value, axis, pairs)  21.4 us
    pallas_call x1, Pallas kernels, run_last(): pl.pallas_call(last_kernel, grid_spec=pltpu.PrefetchScalarGridSpec(num_sc...  13.2 us
    all_to_all x1, starting transfers between devices, body(): amps = routed(first)  8.63 us
    all_to_all x1, starting transfers between devices, body(): more = routed(rest)  7.15 us
    pallas_call x1, Pallas kernels, prep(): pl.pallas_call(prep_kernel, grid_spec=pltpu.PrefetchScalarGridSpec(num_sc...  6.15 us
    unnamed x21, local copies, waits for them, and re-layouts  5.56 us
  transfers between devices with their start and end apart: 10, of which 8 were waited for; matrix products, arithmetic and copies ran while one was open for 2% of the time, Pallas kernels for 23%

commit v1 on v0

--- a/solution.py
+++ b/solution.py
@@ -376,9 +376,10 @@
             east_ref[part] = half_sum(part, PANELS - 1, slice(0, EXTENT)).astype(BF16)
             for j in range(TILE // 128):
                 lanes = slice(128 * j, 128 * j + 128)
-                top_ref[part, :, lanes] = half_sum(part, j + 1, slice(0, HALF))
+                top_ref[part, :, lanes] = half_sum(part, j + 1, slice(0, HALF)).astype(BF16)
                 inner_ref[part, :, lanes] = half_sum(part, j + 1, slice(HALF, HALF + TILE))
-                bottom_ref[part, :, lanes] = half_sum(part, j + 1, slice(HALF + TILE, EXTENT))
+                rows = slice(HALF + TILE, EXTENT)
+                bottom_ref[part, :, lanes] = half_sum(part, j + 1, rows).astype(BF16)
 
 
 def whole(shape):
@@ -425,7 +426,7 @@
             jax.ShapeDtypeStruct(WIDE, F32),
             jax.ShapeDtypeStruct((amps.shape[0], 2, FRAME, FRAME), BF16),
         ],
-        compiler_params=pltpu.CompilerParams(vmem_limit_bytes=56 << 20),
+        compiler_params=pltpu.CompilerParams(vmem_limit_bytes=50 << 20),
         cost_estimate=pl.CostEstimate(
             flops=2 * amps.shape[0] * 16 * FRAME**3, bytes_accessed=24 << 20, transcendentals=0
         ),
@@ -464,8 +465,8 @@
                 pltpu.VMEM(DEEP, BF16),
             ],
         ),
-        out_shape=[jax.ShapeDtypeStruct(s, d) for s, d in zip(shapes, (BF16, BF16, F32, F32, F32))],
-        compiler_params=pltpu.CompilerParams(vmem_limit_bytes=56 << 20),
+        out_shape=[jax.ShapeDtypeStruct(s, d) for s, d in zip(shapes, (BF16,) * 4 + (F32,))],
+        compiler_params=pltpu.CompilerParams(vmem_limit_bytes=54 << 20),
         cost_estimate=pl.CostEstimate(
             flops=amps.shape[0] * 8 * FRAME**3, bytes_accessed=20 << 20, transcendentals=0
         ),
@@ -477,9 +478,9 @@
     for base, west, east, out in (
         (top_ref, west_n, east_n, north_ref), (bottom_ref, west_s, east_s, south_ref)
     ):
-        out[:, :, 0:HALF] = (base[:, :, 0:HALF] + west[...].astype(F32)).astype(BF16)
-        out[:, :, HALF : TILE - HALF] = base[:, :, HALF : TILE - HALF].astype(BF16)
-        out[:, :, TILE - HALF :] = (base[:, :, TILE - HALF :] + east[...].astype(F32)).astype(BF16)
+        out[:, :, 0:HALF] = (base[:, :, 0:HALF].astype(F32) + west[...].astype(F32)).astype(BF16)
+        out[:, :, HALF : TILE - HALF] = base[:, :, HALF : TILE - HALF]
+        out[:, :, TILE - HALF :] = (base[:, :, TILE - HALF :].astype(F32) + east[...].astype(F32)).astype(BF16)
 
 
 def across(top, bottom, from_west, from_east):
@@ -493,7 +494,7 @@
         in_specs=[full, full, first, last, first, last],
         out_specs=[full, full],
         out_shape=[jax.ShapeDtypeStruct((2, HALF, TILE), BF16)] * 2,
-        compiler_params=pltpu.CompilerParams(vmem_limit_bytes=10 << 20),
+        compiler_params=pltpu.CompilerParams(vmem_limit_bytes=50 << 20),
         name="across",
     )(top, bottom, from_west, from_west, from_east, from_east)
 
@@ -529,7 +530,7 @@
         out_specs=pl.BlockSpec(block, place),
         out_shape=jax.ShapeDtypeStruct(base.shape, F32),
         input_output_aliases={0: 0},
-        compiler_params=pltpu.CompilerParams(vmem_limit_bytes=10 << 20),
+        compiler_params=pltpu.CompilerParams(vmem_limit_bytes=50 << 20),
         name="ends",
     )(base, low, high)
 

time: 143 us -> 139 us (0.972)
  the two profiles are of different devices: /device:TPU:71 before, /device:TPU:74 now
where the time goes in v1:
time: 139 us; the launch traced here: 138 us
  waiting for transfers between devices  54.6 us (39%)
  starting transfers between devices  40.6 us (29%)
  Pallas kernels  37.2 us (27%)
  local copies, waits for them, and re-layouts  3.64 us (3%)
  other arithmetic  1.84 us (1%)
    ppermute x8, waiting for transfers between devices, shifted(): return lax.ppermute(value, axis, pairs)  46.9 us
    ppermute x8, starting transfers between devices, shifted(): return lax.ppermute(value, axis, pairs)  29.6 us
    pallas_call x1, Pallas kernels, run_first(): pl.pallas_call(first_kernel, grid_spec=pltpu.PrefetchScalarGridSpec(num_s...  19.5 us
    all_to_all x1, waiting for transfers between devices, body(): more = routed(rest)  7.68 us
    pallas_call x1, Pallas kernels, run_last(): pl.pallas_call(last_kernel, grid_spec=pltpu.PrefetchScalarGridSpec(num_sc...  7.32 us
    all_to_all x1, starting transfers between devices, body(): amps = routed(first)  6.49 us
    pallas_call x1, Pallas kernels, prep(): pl.pallas_call(prep_kernel, grid_spec=pltpu.PrefetchScalarGridSpec(num_sc...  6.15 us
    all_to_all x1, starting transfers between devices, body(): more = routed(rest)  4.47 us
  transfers between devices with their start and end apart: 10, of which 7 were waited for; matrix products, arithmetic and copies ran while one was open for 1% of the time, Pallas kernels for 20%

profile of v1, /device:TPU:74, one launch (start us, length us, event | category | flops | bytes accessed | tf_op | source)
XLA Modules:
  0.0 138.1 jit_solution(9213553763684059525)
XLA Ops:
  0.0 0.0 copy-start.5
  0.0 0.0 copy-start.6
  0.0 1.8 %convert.8 = bf16[2,512,512]{2,1,0:T(8,128)(2,1)S(1)} convert(f32[2,512,512]{2,1,0:T(8,128)} %obj_hbm.1) | non-fusion elementwise | flops 524288 | bytes 3145728 | tf_op jit(solution)/shard_map/convert.5
  1.8 2.4 %collective-permute-start.1 = (bf16[2,128,512]{2,1,0:T(8,128)(2,1)S(1)}, bf16[2,128,512]{2,1,0:T(8,128)(2,1)S(1)}, u32[]{:S(2)}, u32[]{:S(2)}) collective-permute-start(bf16[2,128,512]{2,1,0:T(8,128)(2,1)S(1)} %get-tuple-element.41), channel_id=1, source_target_pairs={{1,0},{2,1},{3,2},{4,3},{5,4},{6,5},{7,6},{9,8},{10,9},{11,10},{12... | collective-permute-start | bytes 786440 | tf_op jit(solution)/shard_map/ppermute | solution.py:541
  4.3 4.3 %collective-permute-start = (bf16[2,128,512]{2,1,0:T(8,128)(2,1)S(1)}, bf16[2,128,512]{2,1,0:T(8,128)(2,1)S(1)}, u32[]{:S(2)}, u32[]{:S(2)}) collective-permute-start(bf16[2,128,512]{2,1,0:T(8,128)(2,1)S(1)} %get-tuple-element.42), channel_id=1, source_target_pairs={{0,1},{1,2},{2,3},{3,4},{4,5},{5,6},{6,7},{8,9},{9,10},{10,11},{11... | collective-permute-start | bytes 786440 | tf_op jit(solution)/shard_map/ppermute | solution.py:541
  8.6 0.0 copy-done.5
  8.6 0.0 copy-done.6
  8.6 0.7 reshape.5.where_ref
  9.3 6.1 %prep.1 = (bf16[16,528,128]{2,1,0:T(8,128)(2,1)}, bf16[16,512,128]{2,1,0:T(8,128)(2,1)}) custom-call(s32[48]{0:T(128)} %reshape.5.where_ref, f32[16,256,256]{2,1,0:T(8,128)} %inten_ref.1, bf16[256,256]{1,0:T(8,128)(2,1)} %constant.6.clone.perm_ref), custom_call_target="tpu_custom_call" | custom-call | flops 536870912 | bytes 6291456 | tf_op jit(solution)/shard_map/prep/pallas_call | solution.py:140
  15.4 0.0 collective-permute-done.1.south_ref
  15.4 1.5 %collective-permute-done.north_ref = bf16[2,128,512]{2,1,0:T(8,128)(2,1)S(1)} collective-permute-done((bf16[2,128,512]{2,1,0:T(8,128)(2,1)S(1)}, bf16[2,128,512]{2,1,0:T(8,128)(2,1)S(1)}, u32[]{:S(2)}, u32[]{:S(2)}) %collective-permute-start) | collective-permute-done | bytes 262176 | tf_op jit(solution)/shard_map/ppermute | solution.py:541
  16.9 6.5 %all-to-all-start = ((bf16[16,528,128]{2,1,0:T(8,128)(2,1)}), bf16[16,528,128]{2,1,0:T(8,128)(2,1)}, u32[]{:S(2)}, u32[]{:S(2)}) async-start(bf16[16,528,128]{2,1,0:T(8,128)(2,1)} %get-tuple-element.23), calls=%async_computation | async-start | bytes 4325376 | tf_op jit(solution)/shard_map/all_to_all | solution.py:553
  23.4 0.1 fusion
  23.6 2.1 %collective-permute-start.2 = (bf16[2,768,128]{2,1,0:T(8,128)(2,1)S(1)}, bf16[2,768,128]{2,1,0:T(8,128)(2,1)S(1)}, u32[]{:S(2)}, u32[]{:S(2)}) collective-permute-start(bf16[2,768,128]{2,1,0:T(8,128)(2,1)S(1)} %pad_maximum_fusion), channel_id=1, source_target_pairs={{0,8},{8,16},{16,24},{24,32},{32,40},{40,48},{48,56},{56,64},{64,7... | collective-permute-start | bytes 1179656 | tf_op jit(solution)/shard_map/ppermute | solution.py:541
  25.7 5.9 %collective-permute-start.3 = (bf16[2,768,128]{2,1,0:T(8,128)(2,1)S(1)}, bf16[2,768,128]{2,1,0:T(8,128)(2,1)S(1)}, u32[]{:S(2)}, u32[]{:S(2)}) collective-permute-start(bf16[2,768,128]{2,1,0:T(8,128)(2,1)S(1)} %pad_maximum_fusion.1), channel_id=1, source_target_pairs={{8,0},{16,8},{24,16},{32,24},{40,32},{48,40},{56,48},{64,56},{72,6... | collective-permute-start | bytes 1179656 | tf_op jit(solution)/shard_map/ppermute | solution.py:541
  31.6 28.7 %collective-permute-done.2.west_ref = bf16[2,768,128]{2,1,0:T(8,128)(2,1)S(1)} collective-permute-done((bf16[2,768,128]{2,1,0:T(8,128)(2,1)S(1)}, bf16[2,768,128]{2,1,0:T(8,128)(2,1)S(1)}, u32[]{:S(2)}, u32[]{:S(2)}) %collective-permute-start.2) | collective-permute-done | bytes 393248 | tf_op jit(solution)/shard_map/ppermute | solution.py:541
  60.3 0.0 collective-permute-done.3.east_ref
  60.3 0.0 copy-start
  60.3 0.0 copy-start.1
  60.3 0.0 all-to-all-done.amp_ref
  60.3 4.5 %all-to-all-start.1 = ((bf16[16,512,128]{2,1,0:T(8,128)(2,1)}), bf16[16,512,128]{2,1,0:T(8,128)(2,1)}, u32[]{:S(2)}, u32[]{:S(2)}) async-start(bf16[16,512,128]{2,1,0:T(8,128)(2,1)} %get-tuple-element.27), calls=%async_computation.1 | async-start | bytes 4194304 | tf_op jit(solution)/shard_map/all_to_all | solution.py:562
  64.8 0.8 slice.82
  65.6 0.1 copy.13
  65.7 0.0 copy-done
  65.8 0.0 copy-done.1
  65.8 0.0 copy-start.4
  65.8 19.5 %first.1 = (f32[2,6,768,128]{3,2,1,0:T(8,128)}, bf16[16,2,256,256]{3,2,1,0:T(8,128)(2,1)}) custom-call(s32[6,16]{1,0:T(8,128)S(1)} %stack.2.meta_ref, bf16[16,528,128]{2,1,0:T(8,128)(2,1)} %all-to-all-done.amp_ref, f32[2,256,256]{2,1,0:T(8,128)S(1)} %copy-done.1, bf16[8,256,256]{2,1,0:T(8,128)(2,1)S(1)} %copy-done, ...), custom_call_target="tpu_custom_call" | custom-call | flops 8589934592 | bytes 25165824 | tf_op jit(solution)/shard_map/first/pallas_call | solution.py:397
  85.3 0.0 copy-done.4
  85.3 7.7 %all-to-all-done.1.amp_ref = bf16[16,512,128]{2,1,0:T(8,128)(2,1)} async-done(((bf16[16,512,128]{2,1,0:T(8,128)(2,1)}), bf16[16,512,128]{2,1,0:T(8,128)(2,1)}, u32[]{:S(2)}, u32[]{:S(2)}) %all-to-all-start.1) | async-done | bytes 2097184 | tf_op jit(solution)/shard_map/all_to_all | solution.py:562
  93.0 7.3 %last.1 = (bf16[2,768,128]{2,1,0:T(8,128)(2,1)}, bf16[2,768,128]{2,1,0:T(8,128)(2,1)}, bf16[2,128,512]{2,1,0:T(8,128)(2,1)}, bf16[2,128,512]{2,1,0:T(8,128)(2,1)}, f32[2,512,512]{2,1,0:T(8,128)}) custom-call(s32[6,16]{1,0:T(8,128)} %copy-done.4, bf16[16,512,128]{2,1,0:T(8,128)(2,1)} %all-to-all-done.1.amp_ref, ...), custom_call_target="tpu_custom_call" | custom-call | flops 2147483648 | bytes 20971520 | tf_op jit(solution)/shard_map/last/pallas_call | solution.py:447
  100.3 7.2 %collective-permute-start.4 = (bf16[2,768,128]{2,1,0:T(8,128)(2,1)}, bf16[2,768,128]{2,1,0:T(8,128)(2,1)S(1)}, u32[]{:S(2)}, u32[]{:S(2)}) collective-permute-start(bf16[2,768,128]{2,1,0:T(8,128)(2,1)} %get-tuple-element.33), channel_id=1, source_target_pairs={{0,8},{8,16},{16,24},{24,32},{32,40},{40,48},{48,56},{56,64},{64,7... | collective-permute-start | bytes 1179656 | tf_op jit(solution)/shard_map/ppermute | solution.py:541
  107.5 1.9 %collective-permute-start.5 = (bf16[2,768,128]{2,1,0:T(8,128)(2,1)}, bf16[2,768,128]{2,1,0:T(8,128)(2,1)S(1)}, u32[]{:S(2)}, u32[]{:S(2)}) collective-permute-start(bf16[2,768,128]{2,1,0:T(8,128)(2,1)} %get-tuple-element.34), channel_id=1, source_target_pairs={{8,0},{16,8},{24,16},{32,24},{40,32},{48,40},{56,48},{64,56},{72,6... | collective-permute-start | bytes 1179656 | tf_op jit(solution)/shard_map/ppermute | solution.py:541
  109.4 4.0 %collective-permute-done.4.west_ref.west_n.west_s = bf16[2,768,128]{2,1,0:T(8,128)(2,1)S(1)} collective-permute-done((bf16[2,768,128]{2,1,0:T(8,128)(2,1)}, bf16[2,768,128]{2,1,0:T(8,128)(2,1)S(1)}, u32[]{:S(2)}, u32[]{:S(2)}) %collective-permute-start.4) | collective-permute-done | bytes 393248 | tf_op jit(solution)/shard_map/ppermute | solution.py:541
  113.5 3.2 %collective-permute-done.5.east_ref.east_n.east_s = bf16[2,768,128]{2,1,0:T(8,128)(2,1)S(1)} collective-permute-done((bf16[2,768,128]{2,1,0:T(8,128)(2,1)}, bf16[2,768,128]{2,1,0:T(8,128)(2,1)S(1)}, u32[]{:S(2)}, u32[]{:S(2)}) %collective-permute-start.5) | collective-permute-done | bytes 393248 | tf_op jit(solution)/shard_map/ppermute | solution.py:541
  116.6 0.0 copy-start.2
  116.6 0.9 copy-done.2
  117.6 0.0 copy-start.3
  117.6 0.9 copy-done.3
  118.5 0.1 across.1
  118.6 3.5 %collective-permute-start.6 = (bf16[2,128,512]{2,1,0:T(8,128)(2,1)S(1)}, bf16[2,128,512]{2,1,0:T(8,128)(2,1)S(1)}, u32[]{:S(2)}, u32[]{:S(2)}) collective-permute-start(bf16[2,128,512]{2,1,0:T(8,128)(2,1)S(1)} %get-tuple-element.37), channel_id=1, source_target_pairs={{0,1},{1,2},{2,3},{3,4},{4,5},{5,6},{6,7},{8,9},{9,10},{10,11},{11... | collective-permute-start | bytes 786440 | tf_op jit(solution)/shard_map/ppermute | solution.py:541
  122.2 2.3 %collective-permute-start.7 = (bf16[2,128,512]{2,1,0:T(8,128)(2,1)S(1)}, bf16[2,128,512]{2,1,0:T(8,128)(2,1)S(1)}, u32[]{:S(2)}, u32[]{:S(2)}) collective-permute-start(bf16[2,128,512]{2,1,0:T(8,128)(2,1)S(1)} %get-tuple-element.38), channel_id=1, source_target_pairs={{1,0},{2,1},{3,2},{4,3},{5,4},{6,5},{7,6},{9,8},{10,9},{11,10},{12... | collective-permute-start | bytes 786440 | tf_op jit(solution)/shard_map/ppermute | solution.py:541
  124.5 2.1 %ends.2.base_ref = f32[2,512,512]{2,1,0:T(8,128)} custom-call(f32[2,512,512]{2,1,0:T(8,128)} %get-tuple-element.32.base_ref, bf16[2,768,128]{2,1,0:T(8,128)(2,1)S(1)} %collective-permute-done.4.west_ref.west_n.west_s, bf16[2,768,128]{2,1,0:T(8,128)(2,1)S(1)} %collective-permute-done.5.east_ref.east_n.east_s), custom_call_target="tpu_custom_call", output_to_operand_aliasing={{}: (0, {})} | custom-call | tf_op jit(solution)/shard_map/ends/pallas_call | solution.py:526
  126.6 2.5 %collective-permute-done.6.north_ref = bf16[2,128,512]{2,1,0:T(8,128)(2,1)S(1)} collective-permute-done((bf16[2,128,512]{2,1,0:T(8,128)(2,1)S(1)}, bf16[2,128,512]{2,1,0:T(8,128)(2,1)S(1)}, u32[]{:S(2)}, u32[]{:S(2)}) %collective-permute-start.6) | collective-permute-done | bytes 262176 | tf_op jit(solution)/shard_map/ppermute | solution.py:541
  129.0 7.1 %collective-permute-done.7.south_ref = bf16[2,128,512]{2,1,0:T(8,128)(2,1)S(1)} collective-permute-done((bf16[2,128,512]{2,1,0:T(8,128)(2,1)S(1)}, bf16[2,128,512]{2,1,0:T(8,128)(2,1)S(1)}, u32[]{:S(2)}, u32[]{:S(2)}) %collective-permute-start.7) | collective-permute-done | bytes 262176 | tf_op jit(solution)/shard_map/ppermute | solution.py:541
  136.1 2.1 %ends.3 = f32[2,512,512]{2,1,0:T(8,128)} custom-call(f32[2,512,512]{2,1,0:T(8,128)} %ends.2.base_ref, bf16[2,128,512]{2,1,0:T(8,128)(2,1)S(1)} %collective-permute-done.6.north_ref, bf16[2,128,512]{2,1,0:T(8,128)(2,1)S(1)} %collective-permute-done.7.south_ref), custom_call_target="tpu_custom_call", output_to_operand_aliasing={{}: (0, {})} | custom-call | tf_op jit(solution)/shard_map/ends/pallas_call | solution.py:526
  (8 shorter events, 0.2 us)
Async XLA Ops:
  0.0 8.6 %copy-start.5 = (s32[16,2]{0,1:T(2,128)S(1)}, s32[16,2]{0,1:T(2,128)}, u32[]{:S(2)}) copy-start(s32[16,2]{0,1:T(2,128)} %param.11) | copy-start | bytes 388
  0.0 8.6 %copy-start.6 = (s32[16,1]{0,1:T(1,128)S(1)}, s32[16,1]{0,1:T(1,128)}, u32[]{:S(2)}) copy-start(s32[16,1]{0,1:T(1,128)} %param.10) | copy-start | bytes 196
  1.8 13.6 %collective-permute-start.1 = (bf16[2,128,512]{2,1,0:T(8,128)(2,1)S(1)}, bf16[2,128,512]{2,1,0:T(8,128)(2,1)S(1)}, u32[]{:S(2)}, u32[]{:S(2)}) collective-permute-start(bf16[2,128,512]{2,1,0:T(8,128)(2,1)S(1)} %get-tuple-element.41), channel_id=1, source_target_pairs={{1,0},{2,1},{3,2},{4,3},{5,4},{6,5},{7,6},{9,8},{10,9},{11,10},{12... | collective-permute-start | bytes 786440 | tf_op jit(solution)/shard_map/ppermute | solution.py:541
  4.3 12.7 %collective-permute-start = (bf16[2,128,512]{2,1,0:T(8,128)(2,1)S(1)}, bf16[2,128,512]{2,1,0:T(8,128)(2,1)S(1)}, u32[]{:S(2)}, u32[]{:S(2)}) collective-permute-start(bf16[2,128,512]{2,1,0:T(8,128)(2,1)S(1)} %get-tuple-element.42), channel_id=1, source_target_pairs={{0,1},{1,2},{2,3},{3,4},{4,5},{5,6},{6,7},{8,9},{9,10},{10,11},{11... | collective-permute-start | bytes 786440 | tf_op jit(solution)/shard_map/ppermute | solution.py:541
  16.9 43.4 %all-to-all-start = ((bf16[16,528,128]{2,1,0:T(8,128)(2,1)}), bf16[16,528,128]{2,1,0:T(8,128)(2,1)}, u32[]{:S(2)}, u32[]{:S(2)}) async-start(bf16[16,528,128]{2,1,0:T(8,128)(2,1)} %get-tuple-element.23), calls=%async_computation | async-start | bytes 4325376 | tf_op jit(solution)/shard_map/all_to_all | solution.py:553
  23.6 36.7 %collective-permute-start.2 = (bf16[2,768,128]{2,1,0:T(8,128)(2,1)S(1)}, bf16[2,768,128]{2,1,0:T(8,128)(2,1)S(1)}, u32[]{:S(2)}, u32[]{:S(2)}) collective-permute-start(bf16[2,768,128]{2,1,0:T(8,128)(2,1)S(1)} %pad_maximum_fusion), channel_id=1, source_target_pairs={{0,8},{8,16},{16,24},{24,32},{32,40},{40,48},{48,56},{56,64},{64,7... | collective-permute-start | bytes 1179656 | tf_op jit(solution)/shard_map/ppermute | solution.py:541
  25.7 34.7 %collective-permute-start.3 = (bf16[2,768,128]{2,1,0:T(8,128)(2,1)S(1)}, bf16[2,768,128]{2,1,0:T(8,128)(2,1)S(1)}, u32[]{:S(2)}, u32[]{:S(2)}) collective-permute-start(bf16[2,768,128]{2,1,0:T(8,128)(2,1)S(1)} %pad_maximum_fusion.1), channel_id=1, source_target_pairs={{8,0},{16,8},{24,16},{32,24},{40,32},{48,40},{56,48},{64,56},{72,6... | collective-permute-start | bytes 1179656 | tf_op jit(solution)/shard_map/ppermute | solution.py:541
  60.3 5.4 %copy-start = (bf16[8,256,256]{2,1,0:T(8,128)(2,1)S(1)}, bf16[8,256,256]{2,1,0:T(8,128)(2,1)}, u32[]{:S(2)}) copy-start(bf16[8,256,256]{2,1,0:T(8,128)(2,1)} %constant.7.clone.table_ref) | copy-start | bytes 3145732
  60.3 5.4 %copy-start.1 = (f32[2,256,256]{2,1,0:T(8,128)S(1)}, f32[2,256,256]{2,1,0:T(8,128)}, u32[]{:S(2)}) copy-start(f32[2,256,256]{2,1,0:T(8,128)} %probe_ref.3) | copy-start | bytes 1572868
  60.3 32.7 %all-to-all-start.1 = ((bf16[16,512,128]{2,1,0:T(8,128)(2,1)}), bf16[16,512,128]{2,1,0:T(8,128)(2,1)}, u32[]{:S(2)}, u32[]{:S(2)}) async-start(bf16[16,512,128]{2,1,0:T(8,128)(2,1)} %get-tuple-element.27), calls=%async_computation.1 | async-start | bytes 4194304 | tf_op jit(solution)/shard_map/all_to_all | solution.py:562
  65.8 19.6 %copy-start.4 = (s32[6,16]{1,0:T(8,128)}, s32[6,16]{1,0:T(8,128)S(1)}, u32[]{:S(2)}) copy-start(s32[6,16]{1,0:T(8,128)S(1)} %stack.2.meta_ref) | copy-start | bytes 1156
  100.3 13.1 %collective-permute-start.4 = (bf16[2,768,128]{2,1,0:T(8,128)(2,1)}, bf16[2,768,128]{2,1,0:T(8,128)(2,1)S(1)}, u32[]{:S(2)}, u32[]{:S(2)}) collective-permute-start(bf16[2,768,128]{2,1,0:T(8,128)(2,1)} %get-tuple-element.33), channel_id=1, source_target_pairs={{0,8},{8,16},{16,24},{24,32},{32,40},{40,48},{48,56},{56,64},{64,7... | collective-permute-start | bytes 1179656 | tf_op jit(solution)/shard_map/ppermute | solution.py:541
  107.5 9.1 %collective-permute-start.5 = (bf16[2,768,128]{2,1,0:T(8,128)(2,1)}, bf16[2,768,128]{2,1,0:T(8,128)(2,1)S(1)}, u32[]{:S(2)}, u32[]{:S(2)}) collective-permute-start(bf16[2,768,128]{2,1,0:T(8,128)(2,1)} %get-tuple-element.34), channel_id=1, source_target_pairs={{8,0},{16,8},{24,16},{32,24},{40,32},{48,40},{56,48},{64,56},{72,6... | collective-permute-start | bytes 1179656 | tf_op jit(solution)/shard_map/ppermute | solution.py:541
  116.6 0.9 copy-start.2
  117.6 0.9 copy-start.3
  118.6 10.4 %collective-permute-start.6 = (bf16[2,128,512]{2,1,0:T(8,128)(2,1)S(1)}, bf16[2,128,512]{2,1,0:T(8,128)(2,1)S(1)}, u32[]{:S(2)}, u32[]{:S(2)}) collective-permute-start(bf16[2,128,512]{2,1,0:T(8,128)(2,1)S(1)} %get-tuple-element.37), channel_id=1, source_target_pairs={{0,1},{1,2},{2,3},{3,4},{4,5},{5,6},{6,7},{8,9},{9,10},{10,11},{11... | collective-permute-start | bytes 786440 | tf_op jit(solution)/shard_map/ppermute | solution.py:541
  122.2 13.9 %collective-permute-start.7 = (bf16[2,128,512]{2,1,0:T(8,128)(2,1)S(1)}, bf16[2,128,512]{2,1,0:T(8,128)(2,1)S(1)}, u32[]{:S(2)}, u32[]{:S(2)}) collective-permute-start(bf16[2,128,512]{2,1,0:T(8,128)(2,1)S(1)} %get-tuple-element.38), channel_id=1, source_target_pairs={{1,0},{2,1},{3,2},{4,3},{5,4},{6,5},{7,6},{9,8},{10,9},{11,10},{12... | collective-permute-start | bytes 786440 | tf_op jit(solution)/shard_map/ppermute | solution.py:541
